TPU v7x, 32 devices: a whole 2x2x4 slice. The times are simulated.
32 devices in a mesh: dp: 16 (over z, y, x), tensor: 2 (over core).
Axes of the slice: x: 2, y: 2, z: 4, core: 2. Of those that a mesh axis runs over, the one named last changes fastest.
Arguments:
- tokens: bfloat16 [16384, 768], P(('dp', 'tensor')), may hold values from -6 to 6
- lengths: int32 [16], P('dp'), may hold values from 1 to 1024, 10240 in all
- qkv_weight: bfloat16 [3, 768, 768], P(None, 'dp', 'tensor'), may hold values from -0.21875 to 0.21875
- qv_bias: float32 [2, 768], P(None, 'tensor'), may hold values from -3 to 3
- out_weight: bfloat16 [768, 768], P('tensor', 'dp'), may hold values from -0.875 to 0.875
- out_bias: float32 [768], replicated, may hold values from -3 to 3
- up_weight: bfloat16 [768, 3072], P('dp', 'tensor'), may hold values from -0.21875 to 0.21875
- up_bias: float32 [3072], P('tensor'), may hold values from -3 to 3
- down_weight: bfloat16 [3072, 768], P('tensor', 'dp'), may hold values from -0.109375 to 0.109375
- down_bias: float32 [768], replicated, may hold values from -3 to 3
- norm1_gain: float32 [768], replicated, may hold values from 0.5 to 1.5
- norm1_shift: float32 [768], replicated, may hold values from -3 to 3
- norm2_gain: float32 [768], replicated, may hold values from 0.5 to 1.5
- norm2_shift: float32 [768], replicated, may hold values from -3 to 3
- cotangent: bfloat16 [16384, 768], P(('dp', 'tensor')), may hold values from -6 to 6
Outputs:
- layer_output: bfloat16 [16384, 768], P(('dp', 'tensor'))
- input_grad: bfloat16 [16384, 768], P(('dp', 'tensor'))
- grad_qkv_weight: float32 [3, 768, 768], P(None, 'dp', 'tensor')
- grad_qv_bias: float32 [2, 768], P(None, 'tensor')
- grad_out_weight: float32 [768, 768], P('tensor', 'dp')
- grad_out_bias: float32 [768], replicated
- grad_up_weight: float32 [768, 3072], P('dp', 'tensor')
- grad_up_bias: float32 [3072], P('tensor')
- grad_down_weight: float32 [3072, 768], P('tensor', 'dp')
- grad_down_bias: float32 [768], replicated
- grad_norm1_gain: float32 [768], replicated
- grad_norm1_shift: float32 [768], replicated
- grad_norm2_gain: float32 [768], replicated
- grad_norm2_shift: float32 [768], replicated
Inputs may be any that keep to these rules, and one draw needn't show every extreme that they name: lengths[s] is the count of real tokens of sequence s; some sequence has 1024.
All inputs are finite; a program needn't handle non-finite values. No bound on the sum of `lengths` on one device may be relied on, other than what follows from the above.
Results may differ from a plain program's by a relative error of at most 0.017.
Values may be sent and summed in bfloat16 or wider, within the bound.
A program may use at most 192 MiB of HBM per device.

v0:
```python
import jax
import jax.numpy as jnp
from jax import lax
from jax.sharding import PartitionSpec as P

HEAD_DIM = 64
LENGTH = 1024
EPSILON = 1e-05
NEGATIVE = -1e30


def layer_norm(values, norm_gain, norm_shift):
    center = values - jnp.mean(values, axis=-1, keepdims=True)
    spread = jnp.mean(center * center, axis=-1, keepdims=True)
    return center * lax.rsqrt(spread + EPSILON) * norm_gain + norm_shift


def gelu_exact(values):
    return jax.nn.gelu(values, approximate=False)


def matmul(left, right):
    return jnp.dot(left, right, preferred_element_type=jnp.float32)


def contract_rows(left, right):
    return lax.dot_general(
        left, right, (((0,), (0,)), ((), ())), preferred_element_type=jnp.float32
    )


def contract_cols(left, right):
    return lax.dot_general(
        left, right, (((1,), (1,)), ((), ())), preferred_element_type=jnp.float32
    )


def per_device(
    tokens,
    lengths,
    qkv_weight,
    qv_bias,
    out_weight,
    out_bias,
    up_weight,
    up_bias,
    down_weight,
    down_bias,
    norm1_gain,
    norm1_shift,
    norm2_gain,
    norm2_shift,
    cotangent,
):
    tok_rows = tokens.shape[0]
    local_width = qkv_weight.shape[2]
    head_count = local_width // HEAD_DIM
    seq_count = lengths.shape[0]
    block_rows = min(512, LENGTH)
    scaling = HEAD_DIM ** (-0.5)
    positions = jnp.arange(LENGTH)
    qkv_full, out_full, up_full, down_full = (
        lax.all_gather(qkv_weight, "dp", axis=1, tiled=True),
        lax.all_gather(out_weight, "dp", axis=1, tiled=True),
        lax.all_gather(up_weight, "dp", axis=0, tiled=True),
        lax.all_gather(down_weight, "dp", axis=1, tiled=True),
    )
    gathered = lax.all_gather(tokens, "tensor", axis=0, tiled=True)
    queries = (matmul(gathered, qkv_full[0]) + qv_bias[0]).astype(jnp.bfloat16)
    key_rows = matmul(gathered, qkv_full[1]).astype(jnp.bfloat16)
    value_rows = (matmul(gathered, qkv_full[2]) + qv_bias[1]).astype(jnp.bfloat16)

    def forward_seq(packed):
        seq_queries, seq_keys, seq_values, length = packed
        query_heads = seq_queries.reshape(LENGTH, head_count, HEAD_DIM)
        key_heads = seq_keys.reshape(LENGTH, head_count, HEAD_DIM)
        value_heads = seq_values.reshape(LENGTH, head_count, HEAD_DIM)
        usable = (positions < length)[None, None, :]
        context_blocks = []
        total_blocks = []
        for block_start in range(0, LENGTH, block_rows):
            block_q = query_heads[block_start : block_start + block_rows]
            scores = (
                jnp.einsum("qhd,khd->hqk", block_q, key_heads, preferred_element_type=jnp.float32)
                * scaling
            )
            scores = jnp.where(usable, scores, NEGATIVE)
            row_top = jnp.max(scores, axis=-1, keepdims=True)
            exponent = jnp.exp(scores - row_top)
            row_total = jnp.sum(exponent, axis=-1, keepdims=True)
            weights = (exponent / row_total).astype(jnp.bfloat16)
            block_context = jnp.einsum(
                "hqk,khd->qhd", weights, value_heads, preferred_element_type=jnp.float32
            )
            context_blocks.append(block_context.reshape(block_rows, local_width))
            total_blocks.append((row_top + jnp.log(row_total))[..., 0])
        return (
            jnp.concatenate(context_blocks, axis=0).astype(jnp.bfloat16),
            jnp.concatenate(total_blocks, axis=1),
        )

    shaped = (
        queries.reshape(seq_count, LENGTH, local_width),
        key_rows.reshape(seq_count, LENGTH, local_width),
        value_rows.reshape(seq_count, LENGTH, local_width),
    )
    contexts, log_totals = lax.map(forward_seq, (shaped[0], shaped[1], shaped[2], lengths))
    context_flat = contexts.reshape(seq_count * LENGTH, local_width)
    row_block = lax.slice_in_dim(context_flat, 0, tok_rows * lax.axis_size("tensor"), axis=0)
    attn = (
        lax.psum_scatter(matmul(row_block, out_full), "tensor", scatter_dimension=0, tiled=True)
        + out_bias
    )
    first_sum = tokens.astype(jnp.float32) + attn
    hidden = layer_norm(first_sum, norm1_gain, norm1_shift)
    hidden_low = hidden.astype(jnp.bfloat16)
    hidden_all = lax.all_gather(hidden_low, "tensor", axis=0, tiled=True)
    upper = matmul(hidden_all, up_full) + up_bias
    active = gelu_exact(upper).astype(jnp.bfloat16)
    row_block = lax.slice_in_dim(active, 0, tok_rows * lax.axis_size("tensor"), axis=0)
    ffn_out = (
        lax.psum_scatter(matmul(row_block, down_full), "tensor", scatter_dimension=0, tiled=True)
        + down_bias
    )
    second_sum = hidden + ffn_out
    layer_output = layer_norm(second_sum, norm2_gain, norm2_shift).astype(jnp.bfloat16)
    qkv_back, out_back, up_back, down_back = (qkv_full, out_full, up_full, down_full)
    unused_two, norm_two_back = jax.vjp(layer_norm, second_sum, norm2_gain, norm2_shift)
    grad_second, gain_two_grad, shift_two_grad = norm_two_back(cotangent.astype(jnp.float32))
    grad_ffn = grad_second.astype(jnp.bfloat16)
    down_bias_grad = jnp.sum(grad_ffn.astype(jnp.float32), axis=0)
    grad_ffn_all = lax.all_gather(grad_ffn, "tensor", axis=0, tiled=True)
    down_weight_grad = contract_rows(active, grad_ffn_all)
    grad_active = contract_cols(grad_ffn_all, down_back)
    unused_gelu, gelu_back = jax.vjp(gelu_exact, upper)
    grad_upper = gelu_back(grad_active)[0].astype(jnp.bfloat16)
    up_bias_grad = jnp.sum(grad_upper.astype(jnp.float32), axis=0)
    up_weight_grad = contract_rows(hidden_all, grad_upper)
    row_block = lax.slice_in_dim(grad_upper, 0, tok_rows * lax.axis_size("tensor"), axis=0)
    grad_hidden = grad_second + lax.psum_scatter(
        contract_cols(row_block, up_back), "tensor", scatter_dimension=0, tiled=True
    )
    unused_one, norm_one_back = jax.vjp(layer_norm, first_sum, norm1_gain, norm1_shift)
    grad_first, gain_one_grad, shift_one_grad = norm_one_back(grad_hidden)
    grad_attn = grad_first.astype(jnp.bfloat16)
    out_bias_grad = jnp.sum(grad_attn.astype(jnp.float32), axis=0)
    grad_attn_all = lax.all_gather(grad_attn, "tensor", axis=0, tiled=True)
    out_weight_grad = contract_rows(context_flat, grad_attn_all)
    grad_context = contract_cols(grad_attn_all, out_back).astype(jnp.bfloat16)

    def backward_seq(packed):
        seq_queries, seq_keys, seq_values, length, seq_grad, seq_totals = packed
        query_heads = seq_queries.reshape(LENGTH, head_count, HEAD_DIM)
        key_heads = seq_keys.reshape(LENGTH, head_count, HEAD_DIM)
        value_heads = seq_values.reshape(LENGTH, head_count, HEAD_DIM)
        usable = (positions < length)[None, None, :]
        key_grad = jnp.zeros((LENGTH, head_count, HEAD_DIM), jnp.float32)
        value_grad = jnp.zeros((LENGTH, head_count, HEAD_DIM), jnp.float32)
        query_blocks = []
        for block_start in range(0, LENGTH, block_rows):
            block_q = query_heads[block_start : block_start + block_rows]
            block_grad = seq_grad[block_start : block_start + block_rows].reshape(
                block_rows, head_count, HEAD_DIM
            )
            scores = (
                jnp.einsum("qhd,khd->hqk", block_q, key_heads, preferred_element_type=jnp.float32)
                * scaling
            )
            scores = jnp.where(usable, scores, NEGATIVE)
            chances = jnp.exp(scores - seq_totals[:, block_start : block_start + block_rows, None])
            weights = chances.astype(jnp.bfloat16)
            value_grad = value_grad + jnp.einsum(
                "hqk,qhd->khd", weights, block_grad, preferred_element_type=jnp.float32
            )
            grad_weights = jnp.einsum(
                "qhd,khd->hqk", block_grad, value_heads, preferred_element_type=jnp.float32
            )
            inner_sum = jnp.sum(grad_weights * chances, axis=-1, keepdims=True)
            grad_scores = (chances * (grad_weights - inner_sum)).astype(jnp.bfloat16)
            block_query_grad = (
                jnp.einsum(
                    "hqk,khd->qhd", grad_scores, key_heads, preferred_element_type=jnp.float32
                )
                * scaling
            )
            query_blocks.append(block_query_grad.reshape(block_rows, local_width))
            key_grad = (
                key_grad
                + jnp.einsum(
                    "hqk,qhd->khd", grad_scores, block_q, preferred_element_type=jnp.float32
                )
                * scaling
            )
        query_grad = jnp.concatenate(query_blocks, axis=0).astype(jnp.bfloat16)
        return (
            query_grad,
            key_grad.reshape(LENGTH, local_width).astype(jnp.bfloat16),
            value_grad.reshape(LENGTH, local_width).astype(jnp.bfloat16),
        )

    grad_shaped = grad_context.reshape(seq_count, LENGTH, local_width)
    query_grads, key_grads, value_grads = lax.map(
        backward_seq, (shaped[0], shaped[1], shaped[2], lengths, grad_shaped, log_totals)
    )
    query_grads = query_grads.reshape(seq_count * LENGTH, local_width)
    key_grads = key_grads.reshape(seq_count * LENGTH, local_width)
    value_grads = value_grads.reshape(seq_count * LENGTH, local_width)
    qv_bias_grad = jnp.stack(
        [
            jnp.sum(query_grads.astype(jnp.float32), axis=0),
            jnp.sum(value_grads.astype(jnp.float32), axis=0),
        ]
    )
    qkv_weight_grad = jnp.stack(
        [
            contract_rows(gathered, query_grads),
            contract_rows(gathered, key_grads),
            contract_rows(gathered, value_grads),
        ]
    )
    part_query = lax.slice_in_dim(query_grads, 0, lax.axis_size("tensor") * tok_rows, axis=0)
    input_grad = (
        grad_first
        + lax.psum_scatter(
            (
                contract_cols(part_query, qkv_back[0])
                + contract_cols(key_grads, qkv_back[1])
                + contract_cols(value_grads, qkv_back[2])
            ).astype(jnp.bfloat16),
            "tensor",
            scatter_dimension=0,
            tiled=True,
        ).astype(jnp.float32)
    ).astype(jnp.bfloat16)
    qkv_grad_own, out_grad_own, up_grad_own, down_grad_own = (
        lax.psum_scatter(qkv_weight_grad, "dp", scatter_dimension=1, tiled=True),
        lax.psum_scatter(out_weight_grad, "dp", scatter_dimension=1, tiled=True),
        lax.psum_scatter(up_weight_grad, "dp", scatter_dimension=0, tiled=True),
        lax.psum_scatter(down_weight_grad, "dp", scatter_dimension=1, tiled=True),
    )
    qv_bias_total, up_bias_total = lax.psum((qv_bias_grad, up_bias_grad), "dp")
    (
        out_bias_total,
        down_bias_total,
        gain_one_total,
        shift_one_total,
        gain_two_total,
        shift_two_total,
    ) = lax.psum(
        (
            out_bias_grad,
            down_bias_grad,
            gain_one_grad,
            shift_one_grad,
            gain_two_grad,
            shift_two_grad,
        ),
        ("dp", "tensor"),
    )
    return (
        layer_output,
        input_grad,
        qkv_grad_own,
        qv_bias_total,
        out_grad_own,
        out_bias_total,
        up_grad_own,
        up_bias_total,
        down_grad_own,
        down_bias_total,
        gain_one_total,
        shift_one_total,
        gain_two_total,
        shift_two_total,
    )


def solution(mesh):
    return jax.shard_map(
        per_device,
        mesh=mesh,
        in_specs=(
            P(("dp", "tensor"), None),
            P("dp"),
            P(None, "dp", "tensor"),
            P(None, "tensor"),
            P("tensor", "dp"),
            P(),
            P("dp", "tensor"),
            P("tensor"),
            P("tensor", "dp"),
            P(),
            P(),
            P(),
            P(),
            P(),
            P(("dp", "tensor"), None),
        ),
        out_specs=(
            P(("dp", "tensor"), None),
            P(("dp", "tensor"), None),
            P(None, "dp", "tensor"),
            P(None, "tensor"),
            P("tensor", "dp"),
            P(),
            P("dp", "tensor"),
            P("tensor"),
            P("tensor", "dp"),
            P(),
            P(),
            P(),
            P(),
            P(),
        ),
        check_vma=False,
    )
```

profile of v0, /device:TPU:0, one launch (start us, length us, event | category | flops | bytes accessed | tf_op | source)
XLA Modules:
  0.0 1038.2 jit_solution(9922317103957784277)
XLA Ops:
  10.1 49.1 %all_gather.26 = bf16[384,768]{0,1:T(8,128)(2,1)} all-gather(bf16[384,48]{0,1:T(8,128)(2,1)} %param.19), channel_id=1, replica_groups=mesh['dp'=16,'tensor'=2] {'dp'}, dimensions={1}, use_global_device_ids=true | all-gather | bytes 626688 | tf_op jit(solution)/shard_map/all_gather | solution.py:64
  59.2 25.9 %all-gather.10.cloned.1.call-done = bf16[3,768,384]{2,1,0:T(8,128)(2,1)} async-done(((bf16[3,48,384]{2,1,0:T(8,128)(2,1)}), bf16[3,768,384]{2,1,0:T(8,128)(2,1)}) %all-gather.10.cloned.1.call-update) | async-done | bytes 1769488 | tf_op jit(solution)/shard_map/all_gather | solution.py:63
  85.1 2.4 add_convert_fusion.5
  87.6 2.2 convolution_convert_fusion.1
  89.8 1.8 fusion.56
  91.6 4.9 fusion.18
  96.6 5.6 fusion
  102.2 1.9 add_convert_fusion.6
  104.2 3.8 fusion.30
  108.0 3.8 fusion.29
  112.5 2.7 fusion.34
  115.9 9.2 reduce-scatter.8.cloned.1.call-done
  125.1 1.7 fusion.53
  129.2 62.5 %all-gather.14.cloned.1.call-done = bf16[768,1536]{1,0:T(8,128)(2,1)} async-done(((bf16[48,1536]{1,0:T(8,128)(2,1)}), bf16[768,1536]{1,0:T(8,128)(2,1)}) %all-gather.14.cloned.1.call-update) | async-done | bytes 2359312 | tf_op jit(solution)/shard_map/all_gather | solution.py:65
  191.6 10.7 %all-gather.12.cloned.1.call-done = bf16[1024,768]{1,0:T(8,128)(2,1)} async-done(((bf16[512,768]{1,0:T(8,128)(2,1)}), bf16[1024,768]{1,0:T(8,128)(2,1)}) %all-gather.12.cloned.1.call-update) | async-done | bytes 1572880 | tf_op jit(solution)/shard_map/all_gather | solution.py:117
  202.3 19.9 %multiply_convert_fusion.2 = (bf16[1024,1536]{1,0:T(8,128)(2,1)}, f32[1024,1536]{1,0:T(8,128)}, f32[1024,1536]{1,0:T(8,128)}) fusion(f32[1536]{0:T(1024)S(1)} %copy-done.44, bf16[1024,768]{1,0:T(8,128)(2,1)} %all-gather.12.cloned.1.call-done, bf16[768,1536]{1,0:T(8,128)(2,1)} %all-gather.14.cloned.1.call-done), kind=kOutput, calls=%fused_computation.24 | convolution fusion | flops 2519728128 | bytes 19666944 | tf_op jit(solution)/shard_map/dot_general | solution.py:23
  222.2 46.7 %all-gather.16.cloned.1.call-done = bf16[1536,768]{0,1:T(8,128)(2,1)} async-done(((bf16[1536,48]{0,1:T(8,128)(2,1)}), bf16[1536,768]{0,1:T(8,128)(2,1)}) %all-gather.16.cloned.1.call-update) | async-done | bytes 2359312 | tf_op jit(solution)/shard_map/all_gather | solution.py:66
  268.8 6.9 fusion.57
  275.8 9.8 reduce-scatter.10.cloned.1.call-done
  285.6 2.0 fusion.51
  291.5 11.1 %all-gather.18.cloned.1.call-done = bf16[1024,768]{1,0:T(8,128)(2,1)} async-done(((bf16[512,768]{1,0:T(8,128)(2,1)}), bf16[1024,768]{1,0:T(8,128)(2,1)}) %all-gather.18.cloned.1.call-update) | async-done | bytes 1572880 | tf_op jit(solution)/shard_map/all_gather | solution.py:132
  302.5 10.9 %convert_reduce_fusion = (f32[1536]{0:T(1024)}, bf16[1024,1536]{1,0:T(8,128)(2,1)S(1)}) fusion(f32[1024,1536]{1,0:T(8,128)} %get-tuple-element.135, f32[1024,1536]{1,0:T(8,128)} %get-tuple-element.146, f32[1536]{0:T(1024)S(1)} %copy-done.44, bf16[1024,768]{1,0:T(8,128)(2,1)} %all-gather.18.cloned.1.call-done, ...), kind=kOutput, calls=%fused_computation.20 | convolution fusion | flops 2442656256 | bytes 19673088 | tf_op jit(solution)/shard_map/dot_general | solution.py:33
  315.1 4.4 fusion.58
  319.5 12.2 %reduce-scatter.12.cloned.1.call-done = f32[512,768]{1,0:T(8,128)} async-done(((f32[1024,768]{1,0:T(8,128)}), f32[512,768]{1,0:T(8,128)}) %reduce-scatter.12.cloned.1.call-update) | async-done | bytes 1572880 | tf_op jit(solution)/shard_map/reduce_scatter | solution.py:140
  331.7 2.8 multiply_reduce_fusion.2
  338.5 10.6 %all-gather.20.cloned.1.call-done = bf16[1024,768]{1,0:T(8,128)(2,1)} async-done(((bf16[512,768]{1,0:T(8,128)(2,1)}), bf16[1024,768]{1,0:T(8,128)(2,1)}) %all-gather.20.cloned.1.call-update) | async-done | bytes 1572880 | tf_op jit(solution)/shard_map/all_gather | solution.py:147
  349.1 2.2 convolution_convert_fusion
  351.4 6.4 fusion.59
  357.9 7.3 fusion.5
  365.1 18.9 %multiply_reduce_fusion.1 = (f32[6,512]{1,0:T(8,128)S(1)}, f32[6,512]{1,0:T(8,128)S(1)}, f32[6,512,1024]{2,1,0:T(8,128)}) fusion(f32[6,512]{1,0:T(8,128)S(1)} %get-tuple-element.151, f32[6,512,1024]{2,1,0:T(8,128)} %copy-done.1, pred[1024]{0:T(1024)(128)(4,1)S(1)} %iota_compare_fusion, f32[6,512,1024]{2,1,0:T(8,128)} %fusion.59, ...), kind=kOutput, calls=%fused_computation.4 | convolution fusion | flops 434104320 | bytes 51561472 | tf_op jit(solution)/shard_map/while/body/eval_jaxpr/qhd,khd->hqk/dot_general | solution.py:175
  384.1 17.3 %multiply_convert_fusion.1 = (bf16[6,512,1024]{2,1,0:T(8,128)(2,1)S(1)}, bf16[6,512,1024]{2,1,0:T(8,128)(2,1)S(1)}) fusion(f32[6,512,1024]{2,1,0:T(8,128)} %get-tuple-element.147, f32[6,512]{1,0:T(8,128)S(1)} %get-tuple-element.107, f32[6,512]{1,0:T(8,128)S(1)} %get-tuple-element.151, f32[6,512,1024]{2,1,0:T(8,128)} %copy-done.1, ...), kind=kLoop, calls=%fused_computation.3 | loop fusion | flops 37748736 | bytes 62964736 | tf_op jit(solution)/shard_map/while/body/eval_jaxpr/convert_element_type | solution.py:179
  401.4 2.0 fusion.27
  405.0 7.2 convert_reduce_fusion.4
  412.2 2.0 fusion.28
  417.9 2.2 add_convert_fusion.1
  420.2 2.3 convolution_bitcast_fusion.2
  424.3 4.1 copy.30
  429.9 6.3 fusion.62
  436.3 1.8 copy-done.18
  438.1 5.8 fusion.61
  445.0 3.5 fusion.33
  449.8 43.9 %all-reduce.1 = (f32[768]{0:T(1024)}, f32[768]{0:T(1024)}, f32[768]{0:T(1024)}, f32[768]{0:T(1024)}, f32[768]{0:T(1024)}, /*index=5*/f32[768]{0:T(1024)}) all-reduce(f32[768]{0:T(1024)S(1)} %copy-done.30, f32[768]{0:T(1024)S(1)} %get-tuple-element.121, f32[768]{0:T(1024)S(1)} %copy-done.32, ...), channel_id=1, replica_groups=mesh['dp'=16,'tensor'=2] {'dp','tensor'}, use_global_device_ids=true, to_apply=%region_24.25 | all-reduce | flops 4608 | bytes 36864 | tf_op jit(solution)/shard_map/psum | solution.py:249
  494.0 76.4 %all-reduce.2 = (f32[2,384]{1,0:T(2,128)}, f32[1536]{0:T(1024)}) all-reduce(f32[2,384]{1,0:T(2,128)S(1)} %pad_maximum_fusion.7, f32[1536]{0:T(1024)S(1)} %copy-done.34), channel_id=1, replica_groups=mesh['dp'=16,'tensor'=2] {'dp'}, use_global_device_ids=true, to_apply=%region_21.22 | all-reduce | flops 2304 | bytes 18432 | tf_op jit(solution)/shard_map/psum | solution.py:241
  570.5 2.3 add_convert_fusion.2
  572.7 45.6 %all-reduce.5.cloned.1.call-done = f32[3,768,384]{2,0,1:T(4,128)} async-done(((f32[3,768,384]{2,0,1:T(4,128)}), f32[3,768,384]{2,0,1:T(4,128)}) %all-reduce.5.cloned.1.call-update) | async-done | bytes 3538960
  620.1 141.2 %reduce-scatter.20.cloned.1.call-done = f32[1536,48]{0,1:T(8,128)} async-done(((f32[1536,768]{0,1:T(8,128)}), f32[1536,48]{0,1:T(8,128)}) %reduce-scatter.20.cloned.1.call-update) | async-done | bytes 294928 | tf_op jit(solution)/shard_map/reduce_scatter | solution.py:239
  761.2 141.7 %reduce-scatter.18.cloned.1.call-done = f32[48,1536]{1,0:T(8,128)} async-done(((f32[768,1536]{1,0:T(8,128)}), f32[48,1536]{1,0:T(8,128)}) %reduce-scatter.18.cloned.1.call-update) | async-done | bytes 294928 | tf_op jit(solution)/shard_map/reduce_scatter | solution.py:238
  902.9 128.6 %reduce-scatter.16.cloned.1.call-done = f32[384,48]{0,1:T(8,128)} async-done(((f32[384,768]{0,1:T(8,128)}), f32[384,48]{0,1:T(8,128)}) %reduce-scatter.16.cloned.1.call-update) | async-done | bytes 73744 | tf_op jit(solution)/shard_map/reduce_scatter | solution.py:237
  (160 shorter events, 27.8 us)
Async XLA Ops:
  7.2 52.0 %all-gather.8.cloned.1.call-start = ((), (), s32[]{:S(2)}) async-start(), calls=%async_computation.7 | async-start | bytes 2359296 | tf_op jit(solution)/shard_map/all_gather | solution.py:68
  7.9 77.2 %all-gather.10.cloned.1.call-start = ((), (), s32[]{:S(2)}) async-start(), calls=%async_computation.8 | async-start | bytes 1880064 | tf_op jit(solution)/shard_map/all_gather | solution.py:63
  8.7 116.4 %reduce-scatter.8.cloned.1.call-start = ((), (), s32[]{:S(2)}) async-start(), calls=%async_computation.9 | async-start | bytes 4718592 | tf_op jit(solution)/shard_map/reduce_scatter | solution.py:111
  59.2 28.3 %copy-start.40 = (bf16[1024,768]{1,0:T(8,128)(2,1)S(1)}, bf16[1024,768]{1,0:T(8,128)(2,1)}, u32[]{:S(2)}) copy-start(bf16[1024,768]{1,0:T(8,128)(2,1)} %all-gather.8.cloned.1.call-done) | copy-start | bytes 4718596
  87.6 4.1 copy-start.6
  87.6 4.1 copy-start.8
  91.6 16.3 %copy-start = (f32[6,512,1024]{2,1,0:T(8,128)}, f32[6,512,1024]{2,1,0:T(8,128)S(1)}, u32[]{:S(2)}) copy-start(f32[6,512,1024]{2,1,0:T(8,128)S(1)} %fusion.56) | copy-start | bytes 37748740
  96.5 7.6 copy-start.1
  96.6 5.7 copy-start.41
  104.1 3.8 copy-start.19
  107.9 3.8 copy-start.24
  108.0 4.5 copy-start.21
  112.5 12.6 %copy-start.16 = (bf16[512,768]{1,0:T(8,128)(2,1)S(1)}, bf16[512,768]{1,0:T(8,128)(2,1)}, u32[]{:S(2)}) copy-start(bf16[512,768]{1,0:T(8,128)(2,1)} %param.15) | copy-start | bytes 2359300
  112.5 12.6 %copy-start.37 = (f32[768]{0:T(1024)S(1)}, f32[768]{0:T(1024)}, u32[]{:S(2)}) copy-start(f32[768]{0:T(1024)} %param.20) | copy-start | bytes 9220
  115.3 11.8 %copy-start.28 = (f32[768]{0:T(1024)S(1)}, f32[768]{0:T(1024)}, u32[]{:S(2)}) copy-start(f32[768]{0:T(1024)} %param.25) | copy-start | bytes 9220
  115.3 11.8 %copy-start.31 = (f32[768]{0:T(1024)S(1)}, f32[768]{0:T(1024)}, u32[]{:S(2)}) copy-start(f32[768]{0:T(1024)} %param.26) | copy-start | bytes 9220
  115.3 76.3 %all-gather.14.cloned.1.call-start = ((), (), s32[]{:S(2)}) async-start(), calls=%async_computation.11 | async-start | bytes 2506752 | tf_op jit(solution)/shard_map/all_gather | solution.py:65
  115.9 86.4 %all-gather.12.cloned.1.call-start = ((), (), s32[]{:S(2)}) async-start(), calls=%async_computation.10 | async-start | bytes 2359296 | tf_op jit(solution)/shard_map/all_gather | solution.py:117
  126.8 75.5 %copy-start.44 = (f32[1536]{0:T(1024)S(1)}, f32[1536]{0:T(1024)}, u32[]{:S(2)}) copy-start(f32[1536]{0:T(1024)} %param.22) | copy-start | bytes 18436
  128.4 140.5 %all-gather.16.cloned.1.call-start = ((), (), s32[]{:S(2)}) async-start(), calls=%async_computation.12 | async-start | bytes 2506752 | tf_op jit(solution)/shard_map/all_gather | solution.py:66
  128.9 156.7 %reduce-scatter.10.cloned.1.call-start = ((), (), s32[]{:S(2)}) async-start(), calls=%async_computation.13 | async-start | bytes 4718592 | tf_op jit(solution)/shard_map/reduce_scatter | solution.py:122
  275.7 9.9 copy-start.38
  275.7 12.2 %copy-start.14 = (bf16[512,768]{1,0:T(8,128)(2,1)S(1)}, bf16[512,768]{1,0:T(8,128)(2,1)}, u32[]{:S(2)}) copy-start(bf16[512,768]{1,0:T(8,128)(2,1)} %param.29) | copy-start | bytes 2359300
  275.8 12.2 %copy-start.29 = (f32[768]{0:T(1024)S(1)}, f32[768]{0:T(1024)}, u32[]{:S(2)}) copy-start(f32[768]{0:T(1024)} %param.27) | copy-start | bytes 9220
  275.8 26.8 %all-gather.18.cloned.1.call-start = ((), (), s32[]{:S(2)}) async-start(), calls=%async_computation.14 | async-start | bytes 2359296 | tf_op jit(solution)/shard_map/all_gather | solution.py:132
  291.4 40.3 %reduce-scatter.12.cloned.1.call-start = ((), (), s32[]{:S(2)}) async-start(), calls=%async_computation.15 | async-start | bytes 4718592 | tf_op jit(solution)/shard_map/reduce_scatter | solution.py:140
  302.5 12.5 %copy-start.39 = (bf16[768,1536]{1,0:T(8,128)(2,1)S(1)}, bf16[768,1536]{1,0:T(8,128)(2,1)}, u32[]{:S(2)}) copy-start(bf16[768,1536]{1,0:T(8,128)(2,1)} %all-gather.14.cloned.1.call-done) | copy-start | bytes 7077892
  319.5 29.7 %all-gather.20.cloned.1.call-start = ((), (), s32[]{:S(2)}) async-start(), calls=%async_computation.16 | async-start | bytes 2359296 | tf_op jit(solution)/shard_map/all_gather | solution.py:147
  334.5 14.6 %copy-start.22 = (bf16[384,768]{0,1:T(8,128)(2,1)S(1)}, bf16[384,768]{0,1:T(8,128)(2,1)}, u32[]{:S(2)}) copy-start(bf16[384,768]{0,1:T(8,128)(2,1)} %all_gather.26) | copy-start | bytes 1769476
  338.0 13.4 %copy-start.20 = (bf16[1024,384]{0,1:T(8,128)(2,1)S(1)}, bf16[1024,384]{0,1:T(8,128)(2,1)}, u32[]{:S(2)}) copy-start(bf16[1024,384]{0,1:T(8,128)(2,1)} %copy-done.19) | copy-start | bytes 2359300
  338.0 232.5 %reduce-scatter.14.cloned.1.call-start = ((), (), s32[]{:S(2)}) async-start(), calls=%async_computation.17 | async-start | bytes 2359296 | tf_op jit(solution)/shard_map/reduce_scatter | solution.py:224
  384.1 17.3 %copy-start.5 = (bf16[1024,384]{0,1:T(8,128)(2,1)S(1)}, bf16[1024,384]{0,1:T(8,128)(2,1)}, u32[]{:S(2)}) copy-start(bf16[1024,384]{0,1:T(8,128)(2,1)} %copy-done.4) | copy-start | bytes 2359300
  403.5 16.7 %copy-start.10 = (bf16[6,64,512]{2,1,0:T(8,128)(2,1)}, bf16[6,64,512]{2,1,0:T(8,128)(2,1)S(1)}, u32[]{:S(2)}) copy-start(bf16[6,64,512]{2,1,0:T(8,128)(2,1)S(1)} %fusion.27) | copy-start | bytes 1179652
  414.3 6.0 copy-start.12
  420.2 198.2 %all-reduce.5.cloned.1.call-start = ((), (), s32[]{:S(2)}) async-start(), calls=%async_computation.21 | async-start | bytes 9437184
  420.2 2.3 copy-start.42
  428.4 332.8 %reduce-scatter.20.cloned.1.call-start = ((), (), s32[]{:S(2)}) async-start(), calls=%async_computation.20 | async-start | bytes 5013504 | tf_op jit(solution)/shard_map/reduce_scatter | solution.py:239
  436.2 466.7 %reduce-scatter.18.cloned.1.call-start = ((), (), s32[]{:S(2)}) async-start(), calls=%async_computation.19 | async-start | bytes 5013504 | tf_op jit(solution)/shard_map/reduce_scatter | solution.py:238
  443.9 4.6 copy-start.45
  443.9 5.9 copy-start.30
  443.9 5.9 copy-start.32
  443.9 5.9 copy-start.33
  443.9 49.8 %copy-start.36 = (f32[6,64]{1,0:T(8,128)S(1)}, f32[6,64]{1,0:T(8,128)}, u32[]{:S(2)}) copy-start(f32[6,64]{1,0:T(8,128)} %get-tuple-element.148) | copy-start | bytes 4612
  443.9 49.9 %copy-start.11 = (bf16[6,64,512]{2,1,0:T(8,128)(2,1)S(1)}, bf16[6,64,512]{2,1,0:T(8,128)(2,1)}, u32[]{:S(2)}) copy-start(bf16[6,64,512]{2,1,0:T(8,128)(2,1)} %copy-done.10) | copy-start | bytes 1179652
  444.0 49.8 %copy-start.13 = (bf16[6,64,512]{2,1,0:T(8,128)(2,1)S(1)}, bf16[6,64,512]{2,1,0:T(8,128)(2,1)}, u32[]{:S(2)}) copy-start(bf16[6,64,512]{2,1,0:T(8,128)(2,1)} %copy-done.12) | copy-start | bytes 1179652
  444.0 50.0 %copy-start.34 = (f32[1536]{0:T(1024)S(1)}, f32[1536]{0:T(1024)}, u32[]{:S(2)}) copy-start(f32[1536]{0:T(1024)} %get-tuple-element.125) | copy-start | bytes 18436
  444.0 126.5 %copy-start.3 = (f32[512,768]{1,0:T(8,128)S(1)}, f32[512,768]{1,0:T(8,128)}, u32[]{:S(2)}) copy-start(f32[512,768]{1,0:T(8,128)} %copy-done.2) | copy-start | bytes 4718596
  444.0 587.5 %reduce-scatter.16.cloned.1.call-start = ((), (), s32[]{:S(2)}) async-start(), calls=%async_computation.18 | async-start | bytes 1253376 | tf_op jit(solution)/shard_map/reduce_scatter | solution.py:237
  (14 other events, 20.4 us)
Sparse Core Ops, SparseCore 0:
  9.6 12.4 all-gather.7
  24.8 60.2 all-gather.9
  115.4 9.6 reduce-scatter.7
  128.1 63.4 all-gather.13
  193.7 8.6 all-gather.11
  205.3 63.4 all-gather.15
  275.9 9.7 reduce-scatter.9
  291.5 10.9 all-gather.17
  319.6 12.0 reduce-scatter.11
  338.1 10.9 all-gather.19
  420.3 10.2 reduce-scatter.13
  436.1 182.1 all-reduce.4
  624.9 136.2 reduce-scatter.19
  766.8 136.0 reduce-scatter.17
  908.8 122.6 reduce-scatter.15
where the time goes:
time: 1050 us; the launch traced here: 1040 us
  waiting for transfers between devices  658 us (63%)
  blocking collectives  169 us (16%)
  matrix products  138 us (13%)
  other arithmetic  39.6 us (4%)
  between operations  16.1 us (2%)
  local copies, waits for them, and re-layouts  15.8 us (2%)
    reduce_scatter x1, waiting for transfers between devices, per_device(): lax.psum_scatter(up_weight_grad, 'dp', scatter_dimension=0, tiled=True)  142 us
    reduce_scatter x1, waiting for transfers between devices, per_device(): lax.psum_scatter(down_weight_grad, 'dp', scatter_dimension=1, tiled=True)  141 us
    reduce_scatter x1, waiting for transfers between devices, per_device(): lax.psum_scatter(out_weight_grad, 'dp', scatter_dimension=1, tiled=True)  129 us
    psum x1, blocking collectives, per_device(): qv_bias_total, up_bias_total = lax.psum((qv_bias_grad, up_bias_grad), 'dp')  76.4 us
    all_gather x1, waiting for transfers between devices, per_device(): lax.all_gather(up_weight, 'dp', axis=0, tiled=True)  62.5 us
    all_gather x1, blocking collectives, per_device(): lax.all_gather(out_weight, 'dp', axis=1, tiled=True)  49.1 us
    unnamed x16, waiting for transfers between devices  48.2 us
    all_gather x1, waiting for transfers between devices, per_device(): lax.all_gather(down_weight, 'dp', axis=1, tiled=True)  46.7 us
  transfers between devices with their start and end apart: 15, of which 13 were waited for; matrix products, arithmetic and copies ran while one was open for 5% of the time, Pallas kernels for 0%

commit v1 on v0

--- a/solution.py
+++ b/solution.py
@@ -2,6 +2,7 @@
 import jax.numpy as jnp
 from jax import lax
 from jax.sharding import PartitionSpec as P
+from jax.lax import all_to_all, psum
 
 HEAD_DIM = 64
 LENGTH = 1024
@@ -52,6 +53,11 @@
     norm2_shift,
     cotangent,
 ):
+
+    def lead_the_spots(mat):
+        carry_out = jnp.stack(psum(1, axis_name="dp") * [mat])
+        return jnp.concatenate(all_to_all(carry_out, "dp", split_axis=0, concat_axis=0), axis=1)
+
     tok_rows = tokens.shape[0]
     local_width = qkv_weight.shape[2]
     head_count = local_width // HEAD_DIM
@@ -61,7 +67,7 @@
     positions = jnp.arange(LENGTH)
     qkv_full, out_full, up_full, down_full = (
         lax.all_gather(qkv_weight, "dp", axis=1, tiled=True),
-        lax.all_gather(out_weight, "dp", axis=1, tiled=True),
+        lead_the_spots(out_weight),
         lax.all_gather(up_weight, "dp", axis=0, tiled=True),
         lax.all_gather(down_weight, "dp", axis=1, tiled=True),
     )

time: 1050 us -> 1050 us (level)
  blocking collectives: 169 us -> 120 us
  waiting for transfers between devices: 658 us -> 697 us
    all_gather x1 -> x0, blocking collectives: 49.1 us -> none  [per_device(): lax.all_gather(out_weight, 'dp', axis=1, tiled=True)]
    all_gather x1, waiting for transfers between devices: 25.9 us -> 62.8 us  [per_device(): lax.all_gather(qkv_weight, 'dp', axis=1, tiled=True)]
  transfers between devices with their start and end apart: 15 -> 16, of which waited for: 13 -> 14; matrix products, arithmetic and copies ran while one was open for 5% -> 8% of each run, Pallas kernels for 0% -> 0%
where the time goes in v1:
time: 1050 us; the launch traced here: 1040 us
  waiting for transfers between devices  697 us (66%)
  matrix products  139 us (13%)
  blocking collectives  120 us (11%)
  other arithmetic  39.6 us (4%)
  local copies, waits for them, and re-layouts  16.7 us (2%)
  between operations  16.2 us (2%)
    reduce_scatter x1, waiting for transfers between devices, per_device(): lax.psum_scatter(up_weight_grad, 'dp', scatter_dimension=0, tiled=True)  142 us
    reduce_scatter x1, waiting for transfers between devices, per_device(): lax.psum_scatter(down_weight_grad, 'dp', scatter_dimension=1, tiled=True)  141 us
    reduce_scatter x1, waiting for transfers between devices, per_device(): lax.psum_scatter(out_weight_grad, 'dp', scatter_dimension=1, tiled=True)  129 us
    psum x1, blocking collectives, per_device(): qv_bias_total, up_bias_total = lax.psum((qv_bias_grad, up_bias_grad), 'dp')  76.4 us
    all_gather x1, waiting for transfers between devices, per_device(): lax.all_gather(qkv_weight, 'dp', axis=1, tiled=True)  62.8 us
    all_gather x1, waiting for transfers between devices, per_device(): lax.all_gather(up_weight, 'dp', axis=0, tiled=True)  62.5 us
    unnamed x16, waiting for transfers between devices  48.2 us
    all_gather x1, waiting for transfers between devices, per_device(): lax.all_gather(down_weight, 'dp', axis=1, tiled=True)  46.7 us
  transfers between devices with their start and end apart: 16, of which 14 were waited for; matrix products, arithmetic and copies ran while one was open for 8% of the time, Pallas kernels for 0%

profile of v1, /device:TPU:0, one launch (start us, length us, event | category | flops | bytes accessed | tf_op | source)
XLA Modules:
  0.0 1038.6 jit_solution(8155375425013341497)
XLA Ops:
  10.3 8.4 all-to-all-start
  20.2 1.9 all-gather.8.cloned.1.call-done
  22.1 62.8 %all-gather.10.cloned.1.call-done = bf16[3,768,384]{2,1,0:T(8,128)(2,1)} async-done(((bf16[3,48,384]{2,1,0:T(8,128)(2,1)}), bf16[3,768,384]{2,1,0:T(8,128)(2,1)}) %all-gather.10.cloned.1.call-update) | async-done | bytes 1769488 | tf_op jit(solution)/shard_map/all_gather | solution.py:69
  84.9 2.4 add_convert_fusion.5
  87.4 2.2 convolution_convert_fusion.1
  89.6 1.8 fusion.56
  91.5 4.9 fusion.18
  96.4 5.6 fusion
  102.0 1.9 add_convert_fusion.6
  104.0 3.8 fusion.30
  107.8 3.8 fusion.29
  111.6 4.0 fusion.34
  116.2 9.2 reduce-scatter.8.cloned.1.call-done
  129.5 62.5 %all-gather.14.cloned.1.call-done = bf16[768,1536]{1,0:T(8,128)(2,1)} async-done(((bf16[48,1536]{1,0:T(8,128)(2,1)}), bf16[768,1536]{1,0:T(8,128)(2,1)}) %all-gather.14.cloned.1.call-update) | async-done | bytes 2359312 | tf_op jit(solution)/shard_map/all_gather | solution.py:71
  191.9 10.7 %all-gather.12.cloned.1.call-done = bf16[1024,768]{1,0:T(8,128)(2,1)} async-done(((bf16[512,768]{1,0:T(8,128)(2,1)}), bf16[1024,768]{1,0:T(8,128)(2,1)}) %all-gather.12.cloned.1.call-update) | async-done | bytes 1572880 | tf_op jit(solution)/shard_map/all_gather | solution.py:123
  202.6 19.9 %multiply_convert_fusion.2 = (bf16[1024,1536]{1,0:T(8,128)(2,1)}, f32[1024,1536]{1,0:T(8,128)}, f32[1024,1536]{1,0:T(8,128)}) fusion(f32[1536]{0:T(1024)S(1)} %copy-done.42, bf16[1024,768]{1,0:T(8,128)(2,1)} %all-gather.12.cloned.1.call-done, bf16[768,1536]{1,0:T(8,128)(2,1)} %all-gather.14.cloned.1.call-done), kind=kOutput, calls=%fused_computation.24 | convolution fusion | flops 2519728128 | bytes 19666944 | tf_op jit(solution)/shard_map/dot_general | solution.py:24
  222.5 46.7 %all-gather.16.cloned.1.call-done = bf16[1536,768]{0,1:T(8,128)(2,1)} async-done(((bf16[1536,48]{0,1:T(8,128)(2,1)}), bf16[1536,768]{0,1:T(8,128)(2,1)}) %all-gather.16.cloned.1.call-update) | async-done | bytes 2359312 | tf_op jit(solution)/shard_map/all_gather | solution.py:72
  269.1 6.9 fusion.57
  276.1 9.8 reduce-scatter.10.cloned.1.call-done
  285.9 2.0 fusion.51
  291.8 11.1 %all-gather.18.cloned.1.call-done = bf16[1024,768]{1,0:T(8,128)(2,1)} async-done(((bf16[512,768]{1,0:T(8,128)(2,1)}), bf16[1024,768]{1,0:T(8,128)(2,1)}) %all-gather.18.cloned.1.call-update) | async-done | bytes 1572880 | tf_op jit(solution)/shard_map/all_gather | solution.py:138
  302.9 10.9 %convert_reduce_fusion = (f32[1536]{0:T(1024)}, bf16[1024,1536]{1,0:T(8,128)(2,1)S(1)}) fusion(f32[1024,1536]{1,0:T(8,128)} %get-tuple-element.149, f32[1024,1536]{1,0:T(8,128)} %get-tuple-element.160, f32[1536]{0:T(1024)S(1)} %copy-done.42, bf16[1024,768]{1,0:T(8,128)(2,1)} %all-gather.18.cloned.1.call-done, ...), kind=kOutput, calls=%fused_computation.20 | convolution fusion | flops 2442656256 | bytes 19673088 | tf_op jit(solution)/shard_map/dot_general | solution.py:34
  315.4 4.4 fusion.58
  319.8 12.2 %reduce-scatter.12.cloned.1.call-done = f32[512,768]{1,0:T(8,128)} async-done(((f32[1024,768]{1,0:T(8,128)}), f32[512,768]{1,0:T(8,128)}) %reduce-scatter.12.cloned.1.call-update) | async-done | bytes 1572880 | tf_op jit(solution)/shard_map/reduce_scatter | solution.py:146
  332.1 2.8 multiply_reduce_fusion.2
  338.8 10.6 %all-gather.20.cloned.1.call-done = bf16[1024,768]{1,0:T(8,128)(2,1)} async-done(((bf16[512,768]{1,0:T(8,128)(2,1)}), bf16[1024,768]{1,0:T(8,128)(2,1)}) %all-gather.20.cloned.1.call-update) | async-done | bytes 1572880 | tf_op jit(solution)/shard_map/all_gather | solution.py:153
  349.5 2.4 convolution_convert_fusion
  351.9 6.4 fusion.59
  358.3 7.3 fusion.5
  365.6 18.9 %multiply_reduce_fusion.1 = (f32[6,512]{1,0:T(8,128)S(1)}, f32[6,512]{1,0:T(8,128)S(1)}, f32[6,512,1024]{2,1,0:T(8,128)}) fusion(f32[6,512]{1,0:T(8,128)S(1)} %get-tuple-element.165, f32[6,512,1024]{2,1,0:T(8,128)} %copy-done.1, pred[1024]{0:T(1024)(128)(4,1)S(1)} %iota_compare_fusion, f32[6,512,1024]{2,1,0:T(8,128)} %fusion.59, ...), kind=kOutput, calls=%fused_computation.4 | convolution fusion | flops 434104320 | bytes 51561472 | tf_op jit(solution)/shard_map/while/body/eval_jaxpr/qhd,khd->hqk/dot_general | solution.py:181
  384.5 17.3 %multiply_convert_fusion.1 = (bf16[6,512,1024]{2,1,0:T(8,128)(2,1)S(1)}, bf16[6,512,1024]{2,1,0:T(8,128)(2,1)S(1)}) fusion(f32[6,512,1024]{2,1,0:T(8,128)} %get-tuple-element.161, f32[6,512]{1,0:T(8,128)S(1)} %get-tuple-element.121, f32[6,512]{1,0:T(8,128)S(1)} %get-tuple-element.165, f32[6,512,1024]{2,1,0:T(8,128)} %copy-done.1, ...), kind=kLoop, calls=%fused_computation.3 | loop fusion | flops 37748736 | bytes 62964736 | tf_op jit(solution)/shard_map/while/body/eval_jaxpr/convert_element_type | solution.py:185
  401.9 2.0 fusion.27
  405.5 7.2 convert_reduce_fusion.4
  412.7 2.0 fusion.28
  418.4 2.2 add_convert_fusion.1
  420.7 2.3 convolution_bitcast_fusion.2
  424.8 4.1 copy.32
  430.3 6.3 fusion.62
  436.7 1.8 copy-done.18
  438.5 5.8 fusion.61
  445.4 3.5 fusion.33
  450.2 43.9 %all-reduce.1 = (f32[768]{0:T(1024)}, f32[768]{0:T(1024)}, f32[768]{0:T(1024)}, f32[768]{0:T(1024)}, f32[768]{0:T(1024)}, /*index=5*/f32[768]{0:T(1024)}) all-reduce(f32[768]{0:T(1024)S(1)} %copy-done.28, f32[768]{0:T(1024)S(1)} %get-tuple-element.135, f32[768]{0:T(1024)S(1)} %copy-done.30, ...), channel_id=1, replica_groups=mesh['dp'=16,'tensor'=2] {'dp','tensor'}, use_global_device_ids=true, to_apply=%region_24.25 | all-reduce | flops 4608 | bytes 36864 | tf_op jit(solution)/shard_map/psum | solution.py:255
  494.5 76.4 %all-reduce.2 = (f32[2,384]{1,0:T(2,128)}, f32[1536]{0:T(1024)}) all-reduce(f32[2,384]{1,0:T(2,128)S(1)} %pad_maximum_fusion.7, f32[1536]{0:T(1024)S(1)} %copy-done.32), channel_id=1, replica_groups=mesh['dp'=16,'tensor'=2] {'dp'}, use_global_device_ids=true, to_apply=%region_21.22 | all-reduce | flops 2304 | bytes 18432 | tf_op jit(solution)/shard_map/psum | solution.py:247
  570.9 2.3 add_convert_fusion.2
  573.1 45.6 %all-reduce.5.cloned.1.call-done = f32[3,768,384]{2,0,1:T(4,128)} async-done(((f32[3,768,384]{2,0,1:T(4,128)}), f32[3,768,384]{2,0,1:T(4,128)}) %all-reduce.5.cloned.1.call-update) | async-done | bytes 3538960
  620.4 141.2 %reduce-scatter.20.cloned.1.call-done = f32[1536,48]{0,1:T(8,128)} async-done(((f32[1536,768]{0,1:T(8,128)}), f32[1536,48]{0,1:T(8,128)}) %reduce-scatter.20.cloned.1.call-update) | async-done | bytes 294928 | tf_op jit(solution)/shard_map/reduce_scatter | solution.py:245
  761.6 141.7 %reduce-scatter.18.cloned.1.call-done = f32[48,1536]{1,0:T(8,128)} async-done(((f32[768,1536]{1,0:T(8,128)}), f32[48,1536]{1,0:T(8,128)}) %reduce-scatter.18.cloned.1.call-update) | async-done | bytes 294928 | tf_op jit(solution)/shard_map/reduce_scatter | solution.py:244
  903.2 128.6 %reduce-scatter.16.cloned.1.call-done = f32[384,48]{0,1:T(8,128)} async-done(((f32[384,768]{0,1:T(8,128)}), f32[384,48]{0,1:T(8,128)}) %reduce-scatter.16.cloned.1.call-update) | async-done | bytes 73744 | tf_op jit(solution)/shard_map/reduce_scatter | solution.py:243
  (158 shorter events, 30.4 us)
Async XLA Ops:
  7.2 14.9 %all-gather.8.cloned.1.call-start = ((), (), s32[]{:S(2)}) async-start(), calls=%async_computation.8 | async-start | bytes 2359296 | tf_op jit(solution)/shard_map/all_gather | solution.py:74
  7.9 77.0 %all-gather.10.cloned.1.call-start = ((), (), s32[]{:S(2)}) async-start(), calls=%async_computation.9 | async-start | bytes 1880064 | tf_op jit(solution)/shard_map/all_gather | solution.py:69
  10.3 101.3 %all-to-all-start = ((bf16[16,384,48]{1,2,0:T(8,128)(2,1)}), bf16[16,384,48]{1,2,0:T(8,128)(2,1)}, u32[]{:S(2)}, u32[]{:S(2)}) async-start(bf16[16,384,48]{1,2,0:T(8,128)(2,1)} %stack.16), calls=%async_computation | async-start | bytes 1179648 | tf_op jit(solution)/shard_map/all_to_all | solution.py:59
  18.7 106.7 %reduce-scatter.8.cloned.1.call-start = ((), (), s32[]{:S(2)}) async-start(), calls=%async_computation.10 | async-start | bytes 4718592 | tf_op jit(solution)/shard_map/reduce_scatter | solution.py:117
  22.1 65.3 %copy-start.38 = (bf16[1024,768]{1,0:T(8,128)(2,1)S(1)}, bf16[1024,768]{1,0:T(8,128)(2,1)}, u32[]{:S(2)}) copy-start(bf16[1024,768]{1,0:T(8,128)(2,1)} %all-gather.8.cloned.1.call-done) | copy-start | bytes 4718596
  87.4 4.0 copy-start.6
  87.4 4.1 copy-start.8
  91.4 16.3 %copy-start = (f32[6,512,1024]{2,1,0:T(8,128)}, f32[6,512,1024]{2,1,0:T(8,128)S(1)}, u32[]{:S(2)}) copy-start(f32[6,512,1024]{2,1,0:T(8,128)S(1)} %fusion.56) | copy-start | bytes 37748740
  96.3 7.6 copy-start.1
  96.4 5.7 copy-start.39
  103.9 3.8 copy-start.19
  107.7 3.8 copy-start.22
  111.5 4.0 copy-start.24
  111.6 13.8 %copy-start.16 = (bf16[512,768]{1,0:T(8,128)(2,1)S(1)}, bf16[512,768]{1,0:T(8,128)(2,1)}, u32[]{:S(2)}) copy-start(bf16[512,768]{1,0:T(8,128)(2,1)} %param.15) | copy-start | bytes 2359300
  111.6 13.8 %copy-start.35 = (f32[768]{0:T(1024)S(1)}, f32[768]{0:T(1024)}, u32[]{:S(2)}) copy-start(f32[768]{0:T(1024)} %param.20) | copy-start | bytes 9220
  115.6 11.8 %copy-start.26 = (f32[768]{0:T(1024)S(1)}, f32[768]{0:T(1024)}, u32[]{:S(2)}) copy-start(f32[768]{0:T(1024)} %param.25) | copy-start | bytes 9220
  115.6 11.8 %copy-start.29 = (f32[768]{0:T(1024)S(1)}, f32[768]{0:T(1024)}, u32[]{:S(2)}) copy-start(f32[768]{0:T(1024)} %param.26) | copy-start | bytes 9220
  115.6 76.3 %all-gather.14.cloned.1.call-start = ((), (), s32[]{:S(2)}) async-start(), calls=%async_computation.12 | async-start | bytes 2506752 | tf_op jit(solution)/shard_map/all_gather | solution.py:71
  116.2 86.4 %all-gather.12.cloned.1.call-start = ((), (), s32[]{:S(2)}) async-start(), calls=%async_computation.11 | async-start | bytes 2359296 | tf_op jit(solution)/shard_map/all_gather | solution.py:123
  127.1 75.5 %copy-start.42 = (f32[1536]{0:T(1024)S(1)}, f32[1536]{0:T(1024)}, u32[]{:S(2)}) copy-start(f32[1536]{0:T(1024)} %param.22) | copy-start | bytes 18436
  128.6 140.5 %all-gather.16.cloned.1.call-start = ((), (), s32[]{:S(2)}) async-start(), calls=%async_computation.13 | async-start | bytes 2506752 | tf_op jit(solution)/shard_map/all_gather | solution.py:72
  129.2 156.7 %reduce-scatter.10.cloned.1.call-start = ((), (), s32[]{:S(2)}) async-start(), calls=%async_computation.14 | async-start | bytes 4718592 | tf_op jit(solution)/shard_map/reduce_scatter | solution.py:128
  276.0 9.9 copy-start.36
  276.1 12.2 %copy-start.14 = (bf16[512,768]{1,0:T(8,128)(2,1)S(1)}, bf16[512,768]{1,0:T(8,128)(2,1)}, u32[]{:S(2)}) copy-start(bf16[512,768]{1,0:T(8,128)(2,1)} %param.29) | copy-start | bytes 2359300
  276.1 12.2 %copy-start.27 = (f32[768]{0:T(1024)S(1)}, f32[768]{0:T(1024)}, u32[]{:S(2)}) copy-start(f32[768]{0:T(1024)} %param.27) | copy-start | bytes 9220
  276.1 26.8 %all-gather.18.cloned.1.call-start = ((), (), s32[]{:S(2)}) async-start(), calls=%async_computation.15 | async-start | bytes 2359296 | tf_op jit(solution)/shard_map/all_gather | solution.py:138
  291.7 40.3 %reduce-scatter.12.cloned.1.call-start = ((), (), s32[]{:S(2)}) async-start(), calls=%async_computation.16 | async-start | bytes 4718592 | tf_op jit(solution)/shard_map/reduce_scatter | solution.py:146
  302.9 12.5 %copy-start.37 = (bf16[768,1536]{1,0:T(8,128)(2,1)S(1)}, bf16[768,1536]{1,0:T(8,128)(2,1)}, u32[]{:S(2)}) copy-start(bf16[768,1536]{1,0:T(8,128)(2,1)} %all-gather.14.cloned.1.call-done) | copy-start | bytes 7077892
  319.8 29.7 %all-gather.20.cloned.1.call-start = ((), (), s32[]{:S(2)}) async-start(), calls=%async_computation.17 | async-start | bytes 2359296 | tf_op jit(solution)/shard_map/all_gather | solution.py:153
  338.3 13.6 %copy-start.20 = (bf16[1024,384]{0,1:T(8,128)(2,1)S(1)}, bf16[1024,384]{0,1:T(8,128)(2,1)}, u32[]{:S(2)}) copy-start(bf16[1024,384]{0,1:T(8,128)(2,1)} %copy-done.19) | copy-start | bytes 2359300
  338.4 232.5 %reduce-scatter.14.cloned.1.call-start = ((), (), s32[]{:S(2)}) async-start(), calls=%async_computation.18 | async-start | bytes 2359296 | tf_op jit(solution)/shard_map/reduce_scatter | solution.py:230
  384.5 17.3 %copy-start.5 = (bf16[1024,384]{0,1:T(8,128)(2,1)S(1)}, bf16[1024,384]{0,1:T(8,128)(2,1)}, u32[]{:S(2)}) copy-start(bf16[1024,384]{0,1:T(8,128)(2,1)} %copy-done.4) | copy-start | bytes 2359300
  403.9 16.7 %copy-start.10 = (bf16[6,64,512]{2,1,0:T(8,128)(2,1)}, bf16[6,64,512]{2,1,0:T(8,128)(2,1)S(1)}, u32[]{:S(2)}) copy-start(bf16[6,64,512]{2,1,0:T(8,128)(2,1)S(1)} %fusion.27) | copy-start | bytes 1179652
  414.7 6.0 copy-start.12
  420.6 198.1 %all-reduce.5.cloned.1.call-start = ((), (), s32[]{:S(2)}) async-start(), calls=%async_computation.22 | async-start | bytes 9437184
  420.7 2.3 copy-start.40
  428.9 332.7 %reduce-scatter.20.cloned.1.call-start = ((), (), s32[]{:S(2)}) async-start(), calls=%async_computation.21 | async-start | bytes 5013504 | tf_op jit(solution)/shard_map/reduce_scatter | solution.py:245
  436.7 466.6 %reduce-scatter.18.cloned.1.call-start = ((), (), s32[]{:S(2)}) async-start(), calls=%async_computation.20 | async-start | bytes 5013504 | tf_op jit(solution)/shard_map/reduce_scatter | solution.py:244
  444.3 4.6 copy-start.43
  444.3 5.9 copy-start.28
  444.4 5.9 copy-start.30
  444.4 5.9 copy-start.31
  444.4 49.8 %copy-start.34 = (f32[6,64]{1,0:T(8,128)S(1)}, f32[6,64]{1,0:T(8,128)}, u32[]{:S(2)}) copy-start(f32[6,64]{1,0:T(8,128)} %get-tuple-element.162) | copy-start | bytes 4612
  444.4 49.9 %copy-start.11 = (bf16[6,64,512]{2,1,0:T(8,128)(2,1)S(1)}, bf16[6,64,512]{2,1,0:T(8,128)(2,1)}, u32[]{:S(2)}) copy-start(bf16[6,64,512]{2,1,0:T(8,128)(2,1)} %copy-done.10) | copy-start | bytes 1179652
  444.4 49.8 %copy-start.13 = (bf16[6,64,512]{2,1,0:T(8,128)(2,1)S(1)}, bf16[6,64,512]{2,1,0:T(8,128)(2,1)}, u32[]{:S(2)}) copy-start(bf16[6,64,512]{2,1,0:T(8,128)(2,1)} %copy-done.12) | copy-start | bytes 1179652
  444.4 50.0 %copy-start.32 = (f32[1536]{0:T(1024)S(1)}, f32[1536]{0:T(1024)}, u32[]{:S(2)}) copy-start(f32[1536]{0:T(1024)} %get-tuple-element.139) | copy-start | bytes 18436
  444.4 126.5 %copy-start.3 = (f32[512,768]{1,0:T(8,128)S(1)}, f32[512,768]{1,0:T(8,128)}, u32[]{:S(2)}) copy-start(f32[512,768]{1,0:T(8,128)} %copy-done.2) | copy-start | bytes 4718596
  444.4 587.4 %reduce-scatter.16.cloned.1.call-start = ((), (), s32[]{:S(2)}) async-start(), calls=%async_computation.19 | async-start | bytes 1253376 | tf_op jit(solution)/shard_map/reduce_scatter | solution.py:243
  (13 other events, 19.6 us)
Sparse Core Ops, SparseCore 0:
  9.6 12.4 all-gather.7
  24.8 60.1 all-gather.9
  115.7 9.6 reduce-scatter.7
  128.4 63.4 all-gather.13
  194.0 8.6 all-gather.11
  205.6 63.4 all-gather.15
  276.2 9.7 reduce-scatter.9
  291.9 10.9 all-gather.17
  319.9 12.0 reduce-scatter.11
  338.5 10.9 all-gather.19
  420.7 10.2 reduce-scatter.13
  436.6 182.0 all-reduce.4
  625.3 136.2 reduce-scatter.19
  767.2 136.0 reduce-scatter.17
  909.1 122.6 reduce-scatter.15
